TPU v7x, 32 devices: a whole 2x2x4 slice. The times are simulated.
32 devices in a mesh: seq: 16 (over z, y, x), fsdp: 2 (over core).
Axes of the slice: x: 2, y: 2, z: 4, core: 2. Of those that a mesh axis runs over, the one named last changes fastest.
Arguments:
- query: bfloat16 [8192, 4096], P('seq', 'fsdp'), may hold values from -6 to 6
- key: bfloat16 [8192, 4096], P('seq', 'fsdp'), may hold values from -6 to 6
- value: bfloat16 [8192, 4096], P('seq', 'fsdp'), may hold values from -16 to 16, as said below
- cotangent: bfloat16 [8192, 4096], P('seq', 'fsdp'), may hold values from -6 to 6
- gain: float32 [4096], P('fsdp'), may hold values from 0.1 to 1.9
Outputs:
- query_grad: bfloat16 [8192, 4096], P('seq', 'fsdp')
- key_grad: bfloat16 [8192, 4096], P('seq', 'fsdp')
- value_grad: bfloat16 [8192, 4096], P('seq', 'fsdp')
- gain_grad: float32 [4096], P('fsdp')
Inputs may be any that keep to these rules, and one draw needn't show every extreme that they name: `value`: values whose typical size differs from head to head.
All inputs are finite; a program needn't handle non-finite values.
Results may differ from a plain program's by a relative error of at most 0.0057.
Values sent between devices are 32-bit elements; how exact they have to be, the bound alone decides.
A program may use at most 128 MiB of HBM per device.

v0:
```python
import math

import jax
import jax.numpy as jnp
from jax import lax
from jax.sharding import PartitionSpec as P

HEAD_DIM = 128
HD = 4096


def prefix_2(part, axis, combine, identity, reverse):
    count = lax.axis_size(axis)
    place = lax.axis_index(axis)
    ahead = count - 1 - place if reverse else place
    gathered = lax.all_gather(part, axis)
    state = jnp.zeros_like(part) + jnp.asarray(identity, part.dtype)

    def one(turn, state):
        source = count - 1 - turn if reverse else turn
        return combine(state, lax.dynamic_index_in_dim(gathered, source, 0, False))

    return lax.fori_loop(0, ahead, one, state)


def add_states(earlier, later):
    return earlier + later


def shards(query, key, value, cotangent, gain):
    rows = query.shape[0]
    width = query.shape[1]
    heads = width // HEAD_DIM
    shape = (rows, heads, HEAD_DIM)
    queries = query.reshape(shape)
    keys = key.reshape(shape)
    values = value.reshape(shape)
    causal = jnp.tril(jnp.ones((rows, rows), dtype=bool))
    own_state = jnp.einsum("tha,thb->hab", keys, values, preferred_element_type=jnp.float32)
    prefix = prefix_2(own_state, "seq", add_states, jnp.zeros_like(own_state), False)
    prefix_low = prefix.astype(jnp.bfloat16)
    scores = jnp.einsum("tha,sha->hts", queries, keys, preferred_element_type=jnp.float32)
    weights = jnp.where(causal[None], scores, 0.0).astype(jnp.bfloat16)
    attended = jnp.einsum("hts,shb->thb", weights, values, preferred_element_type=jnp.float32)
    attended = attended + jnp.einsum(
        "tha,hab->thb", queries, prefix_low, preferred_element_type=jnp.float32
    )
    attended = attended.reshape(rows, width)
    squares = lax.psum(jnp.sum(attended * attended, axis=-1), "fsdp")
    inv_rms = lax.rsqrt(squares / HD + 1e-05)[:, None]
    normed = attended * inv_rms
    upstream = cotangent.astype(jnp.float32)
    partial_gain = jnp.sum(upstream * normed, axis=0)
    scaled = upstream * gain
    crossed = lax.psum(jnp.sum(scaled * normed, axis=-1), "fsdp")
    attended_grad = (scaled - normed * (crossed / HD)[:, None]) * inv_rms
    grads = attended_grad.astype(jnp.bfloat16).reshape(shape)
    own_grad = jnp.einsum("tha,thb->hab", queries, grads, preferred_element_type=jnp.float32)
    suffix = prefix_2(own_grad, "seq", add_states, jnp.zeros_like(own_grad), True)
    suffix_low = suffix.astype(jnp.bfloat16)
    score_grad = jnp.einsum("thb,shb->hts", grads, values, preferred_element_type=jnp.float32)
    score_grad = jnp.where(causal[None], score_grad, 0.0).astype(jnp.bfloat16)
    query_grad = jnp.einsum("hts,sha->tha", score_grad, keys, preferred_element_type=jnp.float32)
    query_grad = query_grad + jnp.einsum(
        "thb,hab->tha", grads, prefix_low, preferred_element_type=jnp.float32
    )
    key_grad = jnp.einsum("hts,tha->sha", score_grad, queries, preferred_element_type=jnp.float32)
    key_grad = key_grad + jnp.einsum(
        "shb,hab->sha", values, suffix_low, preferred_element_type=jnp.float32
    )
    value_grad = jnp.einsum("hts,thb->shb", weights, grads, preferred_element_type=jnp.float32)
    value_grad = value_grad + jnp.einsum(
        "sha,hab->shb", keys, suffix_low, preferred_element_type=jnp.float32
    )
    factor = 1.0 / math.sqrt(rows * lax.axis_size("seq"))
    total_gain = lax.psum(partial_gain, "seq")
    out_shape = (rows, width)
    return (
        query_grad.reshape(out_shape).astype(jnp.bfloat16),
        key_grad.reshape(out_shape).astype(jnp.bfloat16),
        value_grad.reshape(out_shape).astype(jnp.bfloat16),
        total_gain * factor,
    )


def solution(mesh):
    in_specs = (P("seq", "fsdp"), P("seq", "fsdp"), P("seq", "fsdp"), P("seq", "fsdp"), P("fsdp"))
    out_specs = (P("seq", "fsdp"), P("seq", "fsdp"), P("seq", "fsdp"), P("fsdp"))
    return jax.shard_map(shards, mesh=mesh, in_specs=in_specs, out_specs=out_specs, check_vma=False)
```

profile of v0, /device:TPU:0, one launch (start us, length us, event | category | flops | bytes accessed | tf_op | source)
XLA Modules:
  0.0 514.0 jit_solution(11441069457535604070)
XLA Ops:
  7.2 3.7 copy.61
  10.9 4.3 copy.35
  15.2 3.9 fusion.13
  19.3 4.1 select_convert_fusion.1
  23.4 3.2 copy-done.1
  26.6 4.8 fusion.8
  31.4 182.2 %all-gather.5.cloned.1.call-done = f32[256,128,128]{2,1,0:T(8,128)} async-done(((f32[16,128,128]{2,1,0:T(8,128)}), f32[256,128,128]{2,1,0:T(8,128)}) %all-gather.5.cloned.1.call-update) | async-done | bytes 16777232 | tf_op jit(solution)/shard_map/all_gather | solution.py:16
  213.7 5.0 multiply_reduce_fusion
  218.7 2.4 psum.21
  221.2 5.4 %copy.39 = f32[512,2048]{1,0:T(8,128)} copy(f32[512,2048]{0,1:T(8,128)} %bitcast.111) | data formatting | bytes 8388608 | tf_op jit(solution)/shard_map/reshape | solution.py:48
  226.6 4.0 fusion.5
  230.6 2.6 psum.22
  233.3 5.1 fusion.4
  238.4 3.9 copy.57
  242.3 3.3 fusion.24
  245.6 2.6 copy.47
  248.2 4.9 select_convert_fusion
  253.1 4.9 fusion.39
  257.9 4.3 fusion.7
  262.2 3.9 copy.52
  266.1 64.2 %psum.23 = f32[2048]{0:T(1024)S(1)} all-reduce(f32[2048]{0:T(1024)S(1)} %get-tuple-element.97), channel_id=1, replica_groups=mesh['seq'=16,'fsdp'=2] {'seq'}, use_global_device_ids=true, to_apply=%region_9.10 | all-reduce | flops 2048 | bytes 16384 | tf_op jit(solution)/shard_map/psum | solution.py:76
  330.9 7.3 %fusion.40 = f32[16,128,512]{2,1,0:T(8,128)} fusion(bf16[512,16,128]{0,2,1:T(8,128)(2,1)} %bitcast.109, bf16[16,512,512]{2,1,0:T(8,128)(2,1)} %copy-done.1), kind=kOutput, calls=%fused_computation.53 | convolution fusion | flops 1073741824 | bytes 14680064 | tf_op jit(solution)/shard_map/hts,thb->shb/dot_general | solution.py:71
  338.2 124.2 %all-gather.7.cloned.1.call-done = f32[256,128,128]{2,1,0:T(8,128)} async-done(((f32[16,128,128]{2,1,0:T(8,128)}), f32[256,128,128]{2,1,0:T(8,128)}) %all-gather.7.cloned.1.call-update) | async-done | bytes 16777232 | tf_op jit(solution)/shard_map/all_gather | solution.py:16
  462.5 22.9 %while.23 = (s32[]{:T(128)}, f32[16,128,128]{2,1,0:T(8,128)S(1)}, s32[]{:T(128)}, f32[16,16,128,128]{3,2,1,0:T(8,128)}, s32[]{:T(128)}, /*index=5*/s32[]{:T(128)}, s32[]{:T(128)}, s32[]{:T(128)}) while((s32[]{:T(128)}, f32[16,128,128]{2,1,0:T(8,128)S(1)}, s32[]{:T(128)}, f32[16,16,128,128]{3,2,1,0:T(8,128)}, s32[]{:T(128)}, ...), condition=%wide.region_7.8_spmd, body=%wide.region_6.7_spmd.sunk | while | flops 262150 | bytes 3145871 | solution.py:23
  462.5 1.5 bitcast_add_fusion.8
  464.0 1.5 bitcast_add_fusion.8
  479.1 1.5 bitcast_add_fusion.8
  485.4 4.4 fusion.10
  489.9 2.2 add_convert_fusion
  492.0 3.9 copy.54
  495.9 7.3 %fusion.6 = bf16[512,16,128]{0,2,1:T(8,128)(2,1)} fusion(f32[16,128,512]{2,1,0:T(8,128)} %fusion.10, bf16[16,512,512]{2,1,0:T(8,128)(2,1)} %copy-done.3, bf16[512,2048]{1,0:T(8,128)(2,1)S(1)} %copy-done), kind=kOutput, calls=%fused_computation.13 | convolution fusion | flops 1075838976 | bytes 16777216 | tf_op jit(solution)/shard_map/hts,tha->sha/dot_general | solution.py:67
  503.3 3.9 copy.53
  (40 shorter events, 18.9 us)
Async XLA Ops:
  7.2 12.1 %copy-start = (bf16[512,2048]{1,0:T(8,128)(2,1)S(1)}, bf16[512,2048]{1,0:T(8,128)(2,1)}, u32[]{:S(2)}) copy-start(bf16[512,2048]{1,0:T(8,128)(2,1)} %param.9) | copy-start | bytes 6291460
  7.2 206.4 %all-gather.5.cloned.1.call-start = ((), (), s32[]{:S(2)}) async-start(), calls=%async_computation | async-start | bytes 17825792 | tf_op jit(solution)/shard_map/all_gather | solution.py:16
  19.1 443.3 %all-gather.7.cloned.1.call-start = ((), (), s32[]{:S(2)}) async-start(), calls=%async_computation.1 | async-start | bytes 17825792 | tf_op jit(solution)/shard_map/all_gather | solution.py:16
  19.3 7.4 %copy-start.5 = (bf16[512,2048]{1,0:T(8,128)(2,1)S(1)}, bf16[512,2048]{1,0:T(8,128)(2,1)}, u32[]{:S(2)}) copy-start(bf16[512,2048]{1,0:T(8,128)(2,1)} %param.11) | copy-start | bytes 6291460
  23.4 3.2 copy-start.1
  221.2 5.4 %copy-start.8 = (f32[2048]{0:T(1024)S(1)}, f32[2048]{0:T(1024)}, u32[]{:S(2)}) copy-start(f32[2048]{0:T(1024)} %param.13) | copy-start | bytes 24580
  248.2 4.9 copy-start.6
  253.0 4.9 copy-start.3
  253.1 4.9 copy-start.2
  485.4 4.5 copy-start.4
  485.4 4.4 copy-start.7
Sparse Core Ops, SparseCore 0:
  19.2 194.3 all-gather.4
  248.3 214.0 all-gather.6
where the time goes:
time: 515 us; the launch traced here: 514 us
  waiting for transfers between devices  306 us (59%)
  blocking collectives  69.3 us (13%)
  matrix products  56.4 us (11%)
  local copies, waits for them, and re-layouts  35 us (7%)
  other arithmetic  32.1 us (6%)
  between operations  14.2 us (3%)
    all_gather x2, waiting for transfers between devices, prefix_2(): gathered = lax.all_gather(part, axis)  306 us
    psum x1, blocking collectives, shards(): total_gain = lax.psum(partial_gain, 'seq')  64.2 us
    add x15, other arithmetic, add_states(): return earlier + later  22.3 us
    unnamed x22, local copies, waits for them, and re-layouts  18.7 us
  transfers between devices with their start and end apart: 2, of which 2 were waited for; matrix products, arithmetic and copies ran while one was open for 7% of the time, Pallas kernels for 0%

commit v1 on v0

v1 whole, which is shorter than its diff:
```python
import functools
import math

import jax
import jax.numpy as jnp
from jax import lax
from jax.experimental import pallas as pl
from jax.experimental.pallas import tpu as pltpu
from jax.sharding import PartitionSpec as P

HEAD_DIM = 128
HD = 4096
EPS = 1e-05
MESH = pl.DeviceIdType.MESH
F32 = jnp.float32
BF16 = jnp.bfloat16


def dot_ab(a, b):
    return lax.dot_general(a, b, (((1,), (0,)), ((), ())), preferred_element_type=F32)


def dot_abt(a, b):
    return lax.dot_general(a, b, (((1,), (1,)), ((), ())), preferred_element_type=F32)


def dot_atb(a, b):
    return lax.dot_general(a, b, (((0,), (0,)), ((), ())), preferred_element_type=F32)


def group_size(count):
    size = 1
    while size * size < count:
        size *= 2
    return size


def lower(block, offset):
    row = lax.broadcasted_iota(jnp.int32, block.shape, 0) + offset
    col = lax.broadcasted_iota(jnp.int32, block.shape, 1)
    return jnp.where(row >= col, block, 0.0).astype(BF16)


def upper(block):
    row = lax.broadcasted_iota(jnp.int32, block.shape, 0)
    col = lax.broadcasted_iota(jnp.int32, block.shape, 1)
    return jnp.where(row <= col, block, 0.0).astype(BF16)


def cols_of(head):
    return pl.ds(pl.multiple_of(head * HEAD_DIM, HEAD_DIM), HEAD_DIM)


class Scan:
    def __init__(self, which, reverse, g, m, chunks, refs, sems):
        self.which, self.reverse, self.g, self.m, self.chunks = which, reverse, g, m, chunks
        self.own, self.slots, self.carry, self.fwd, self.outs, self.result = refs
        self.a_send, self.a_recv, self.z_send, self.z_recv, self.b_send, self.b_recv = sems
        me = lax.axis_index("seq")
        self.z, self.i = me // g, lax.rem(me, g)
        self.piece = self.own.shape[0] // g
        self.ch = self.piece // chunks

    def peer(self, d):
        return lax.rem(self.i + d, self.g)

    def rows(self, p, j):
        return pl.ds(pl.multiple_of(p * self.piece + j * self.ch, self.ch), self.ch)

    def part(self, j):
        return pl.ds(j * self.ch, self.ch)

    def spread(self, d, j, arriving=False):
        p = self.peer(d)
        slot = p if arriving else self.i
        return pltpu.make_async_remote_copy(
            src_ref=self.own.at[self.rows(p, j)],
            dst_ref=self.slots.at[slot, self.part(j)],
            send_sem=self.a_send.at[self.which, d, j],
            recv_sem=self.a_recv.at[self.which, slot, j],
            device_id={"seq": self.z * self.g + p},
            device_id_type=MESH,
        )

    def chain(self, j):
        nearer = self.z - 1 if self.reverse else self.z + 1
        target = jnp.clip(nearer, 0, self.m - 1)
        return pltpu.make_async_remote_copy(
            src_ref=self.fwd.at[self.part(j)],
            dst_ref=self.carry.at[self.part(j)],
            send_sem=self.z_send.at[self.which, j],
            recv_sem=self.z_recv.at[self.which, j],
            device_id={"seq": target * self.g + self.i},
            device_id_type=MESH,
        )

    def hand(self, d, j, arriving=False):
        p = self.peer(d)
        owner = p if arriving else self.i
        return pltpu.make_async_remote_copy(
            src_ref=self.outs.at[p, self.part(j)],
            dst_ref=self.result.at[self.rows(owner, j)],
            send_sem=self.b_send.at[self.which, d, j],
            recv_sem=self.b_recv.at[self.which, owner, j],
            device_id={"seq": self.z * self.g + p},
            device_id_type=MESH,
        )

    def first(self):
        return self.z == (self.m - 1 if self.reverse else 0)

    def last(self):
        return self.z == (0 if self.reverse else self.m - 1)

    def process(self, j):
        part = self.part(j)
        for d in range(1, self.g):
            self.spread(d, j, True).wait_recv()
        total = self.slots[0, part]
        for p in range(1, self.g):
            total = total + self.slots[p, part]

        @pl.when(self.first())
        def _():
            self.carry[part] = jnp.zeros_like(total)

        @pl.when(jnp.logical_not(self.first()))
        def _():
            self.chain(j).wait_recv()

        @pl.when(jnp.logical_not(self.last()))
        def _():
            self.fwd[part] = self.carry[part] + total
            self.chain(j).start()

        running = self.carry[part]
        order = range(self.g)
        for p in reversed(order) if self.reverse else order:
            self.outs[p, part] = running
            running = running + self.slots[p, part]
        for d in range(1, self.g):
            self.hand(d, j).start()
        self.result[self.rows(self.i, j)] = self.outs[self.i, part]

    def drain(self):
        for j in range(self.chunks):
            for d in range(1, self.g):
                self.spread(d, j).wait_send()
                self.hand(d, j).wait_send()

            @pl.when(jnp.logical_not(self.last()))
            def _():
                self.chain(j).wait_send()


def kernel(
    n, g, fs, chunks, groups,
    q_hbm, k_hbm, v_hbm, c_hbm, gain_ref,
    qg_hbm, kg_hbm, vg_hbm, gg_ref,
    q, k, v, cot, do, att, kg_l, vg_l, qg, kg, vg,
    own, slots, carry, fwd, outs, result,
    sq, cr, stats, gp, gz,
    in_sem, out_sem, a_send, a_recv, z_send, z_recv, b_send, b_recv,
    f_send, f_recv, g_send, g_recv, h_send, h_recv,
):
    rows, width = q.shape
    heads = width // HEAD_DIM
    half = rows // 2
    m = n // g
    me = lax.axis_index("seq")
    mine = lax.axis_index("fsdp")
    z, i = me // g, lax.rem(me, g)

    loads = [
        pltpu.make_async_copy(src, dst, in_sem.at[at])
        for at, (src, dst) in enumerate(((k_hbm, k), (v_hbm, v), (q_hbm, q), (c_hbm, cot)))
    ]
    for load in loads:
        load.start()

    barrier = pltpu.get_barrier_semaphore()
    for d in range(1, g):
        pl.semaphore_signal(
            barrier, inc=1, device_id={"seq": z * g + lax.rem(i + d, g)}, device_id_type=MESH
        )
    for d in range(1, m):
        pl.semaphore_signal(
            barrier, inc=1, device_id={"seq": lax.rem(z + d, m) * g + i}, device_id_type=MESH
        )
    for d in range(1, fs):
        pl.semaphore_signal(
            barrier, inc=1, device_id={"fsdp": lax.rem(mine + d, fs)}, device_id_type=MESH
        )

    sems = (a_send, a_recv, z_send, z_recv, b_send, b_recv)
    scans = [
        Scan(w, w == 1, g, m, chunks, tuple(r.at[w] for r in (own, slots, carry, fwd, outs, result)), sems)
        for w in range(2)
    ]
    per = heads // g

    def head_order(turn):
        if per:
            for j in range(chunks):
                for d in range(g):
                    turn(lax.rem(i + d, g) * per + j, d, j)

    def make_states(scan, state_of):
        def turn(head, d, j):
            state = state_of(head)
            if d == 0:
                scan.slots[i, scan.part(j)] = state
            else:
                scan.own[scan.rows(scan.peer(d), j)] = state
                scan.spread(d, j).start()

        if per:
            for j in range(chunks):
                for d in list(range(1, g)) + [0]:
                    turn(lax.rem(i + d, g) * per + j, d, j)
        else:
            for head in range(heads):
                scan.own[pl.ds(head * HEAD_DIM, HEAD_DIM)] = state_of(head)
            for j in range(chunks):
                scan.slots[i, scan.part(j)] = scan.own[scan.rows(i, j)]
                for d in range(1, g):
                    scan.spread(d, j).start()

    def arrivals(scan, visit):
        if per:
            for j in range(chunks):
                for d in range(g):
                    if d:
                        scan.hand(d, j, True).wait_recv()
                    visit(lax.rem(i + d, g) * per + j)
        else:
            for j in range(chunks):
                for d in range(1, g):
                    scan.hand(d, j, True).wait_recv()
            for head in range(heads):
                visit(head)

    def state_at(scan, head):
        at = pl.ds(pl.multiple_of(head * HEAD_DIM, HEAD_DIM), HEAD_DIM)
        return scan.result[at].astype(BF16)

    loads[0].wait()
    loads[1].wait()
    pl.semaphore_wait(barrier, (g - 1) + (m - 1) + (fs - 1))
    make_states(scans[0], lambda head: dot_atb(k[:, cols_of(head)], v[:, cols_of(head)]))
    loads[2].wait()

    top, low = pl.ds(0, half), pl.ds(half, half)

    def inside(head, _):
        cols = cols_of(head)
        kh, vh = k[:, cols], v[:, cols]
        w0 = lower(dot_abt(q[top, cols], k[top, cols]), 0)
        w1 = lower(dot_abt(q[low, cols], kh), half)
        att[top, cols] = dot_ab(w0, v[top, cols])
        att[low, cols] = dot_ab(w1, vh)
        return 0

    for j in range(chunks):
        lax.fori_loop(groups[j], groups[j + 1], inside, 0)
        scans[0].process(j)
    lax.fori_loop(groups[chunks], heads, inside, 0)
    loads[3].wait()

    sq[...] = jnp.zeros_like(sq)
    cr[...] = jnp.zeros_like(cr)

    def finish(head):
        cols = cols_of(head)
        a = att[:, cols] + dot_ab(q[:, cols], state_at(scans[0], head))
        att[:, cols] = a
        sq[...] += a * a
        cr[...] += a * (cot[:, cols].astype(F32) * gain_ref[:, cols])

    arrivals(scans[0], finish)

    lane = lax.broadcasted_iota(jnp.int32, sq.shape, 1)
    stats[mine] = jnp.where(
        lane < HEAD_DIM // 2,
        jnp.sum(sq[...], axis=1, keepdims=True),
        jnp.sum(cr[...], axis=1, keepdims=True),
    )

    def share(d, slot):
        return pltpu.make_async_remote_copy(
            src_ref=stats.at[mine],
            dst_ref=stats.at[slot],
            send_sem=f_send.at[d],
            recv_sem=f_recv.at[slot],
            device_id={"fsdp": lax.rem(mine + d, fs)},
            device_id_type=MESH,
        )

    for d in range(1, fs):
        share(d, mine).start()
    for d in range(1, fs):
        share(d, lax.rem(mine + d, fs)).wait_recv()
    both = stats[0]
    for f in range(1, fs):
        both = both + stats[f]
    inv = lax.rsqrt(both[:, 0:1] / HD + EPS)
    mean = both[:, HEAD_DIM - 1 : HEAD_DIM] * inv / HD
    sq[...] = jnp.broadcast_to(inv, sq.shape)
    cr[...] = jnp.broadcast_to(mean, cr.shape)

    def grad_state(head):
        cols = cols_of(head)
        up = cot[:, cols].astype(F32)
        normed = att[:, cols] * sq[...]
        gp[i, :, cols] = jnp.sum(up * normed, axis=0, keepdims=True)
        d_h = ((up * gain_ref[:, cols] - normed * cr[...]) * sq[...]).astype(BF16)
        do[:, cols] = d_h
        return dot_atb(q[:, cols], d_h)

    make_states(scans[1], grad_state)

    def gain_near(d, slot):
        return pltpu.make_async_remote_copy(
            src_ref=gp.at[i],
            dst_ref=gp.at[slot],
            send_sem=g_send.at[d],
            recv_sem=g_recv.at[slot],
            device_id={"seq": z * g + lax.rem(i + d, g)},
            device_id_type=MESH,
        )

    def gain_far(d, slot):
        return pltpu.make_async_remote_copy(
            src_ref=gz.at[z],
            dst_ref=gz.at[slot],
            send_sem=h_send.at[d],
            recv_sem=h_recv.at[slot],
            device_id={"seq": lax.rem(z + d, m) * g + i},
            device_id_type=MESH,
        )

    for d in range(1, g):
        gain_near(d, i).start()

    def backward(head, _):
        cols = cols_of(head)
        qh, kh, vh, dh = q[:, cols], k[:, cols], v[:, cols], do[:, cols]
        q1, k0, v0, d1 = q[low, cols], k[top, cols], v[top, cols], do[low, cols]
        from_prefix = dot_abt(dh, state_at(scans[0], head))
        s0 = lower(dot_abt(do[top, cols], v0), 0)
        s1 = lower(dot_abt(d1, vh), half)
        qg[top, cols] = (dot_ab(s0, k0) + from_prefix[:half]).astype(BF16)
        qg[low, cols] = (dot_ab(s1, kh) + from_prefix[half:]).astype(BF16)
        t0 = upper(dot_abt(v0, dh))
        t1 = upper(dot_abt(v[low, cols], d1))
        kg_l[top, cols] = dot_ab(t0, qh)
        kg_l[low, cols] = dot_ab(t1, q1)
        w0 = upper(dot_abt(k0, qh))
        w1 = upper(dot_abt(k[low, cols], q1))
        vg_l[top, cols] = dot_ab(w0, dh)
        vg_l[low, cols] = dot_ab(w1, d1)
        return 0

    for j in range(chunks):
        lax.fori_loop(groups[j], groups[j + 1], backward, 0)
        scans[1].process(j)
    lax.fori_loop(groups[chunks], heads, backward, 0)
    store_q = pltpu.make_async_copy(qg, qg_hbm, out_sem.at[0, 0])
    store_q.start()

    for d in range(1, g):
        gain_near(d, lax.rem(i + d, g)).wait_recv()
    near = gp[0]
    for p in range(1, g):
        near = near + gp[p]
    gz[z] = near
    for d in range(1, m):
        gain_far(d, z).start()

    def store(at, src, dst, head):
        cols = cols_of(head)
        return pltpu.make_async_copy(src.at[:, cols], dst.at[:, cols], out_sem.at[at, head])

    def last(head):
        cols = cols_of(head)
        suffix = state_at(scans[1], head)
        kg[:, cols] = (kg_l[:, cols] + dot_abt(v[:, cols], suffix)).astype(BF16)
        vg[:, cols] = (vg_l[:, cols] + dot_ab(k[:, cols], suffix)).astype(BF16)
        store(1, kg, kg_hbm, head).start()
        store(2, vg, vg_hbm, head).start()

    arrivals(scans[1], last)

    for d in range(1, m):
        gain_far(d, lax.rem(z + d, m)).wait_recv()
    total = gz[0]
    for p in range(1, m):
        total = total + gz[p]
    gg_ref[...] = total * (1.0 / math.sqrt(rows * n))

    for scan in scans:
        scan.drain()
    for d in range(1, fs):
        share(d, mine).wait_send()
    for d in range(1, g):
        gain_near(d, i).wait_send()
    for d in range(1, m):
        gain_far(d, z).wait_send()
    store_q.wait()

    def stored(head, _):
        store(1, kg, kg_hbm, head).wait()
        store(2, vg, vg_hbm, head).wait()
        return 0

    lax.fori_loop(0, heads, stored, 0)


def solution(mesh):
    n, fs = mesh.shape["seq"], mesh.shape["fsdp"]
    g = group_size(n)
    m = n // g

    def shards(query, key, value, cotangent, gain):
        rows, width = query.shape
        heads = width // HEAD_DIM
        chunks = max(heads // g, 1)
        state = heads * HEAD_DIM
        piece = state // g
        step = heads // (chunks + 1)
        groups = tuple(min(heads, (j * heads) // (chunks + 1)) for j in range(chunks + 1))
        any_space = pl.BlockSpec(memory_space=pl.ANY)
        vmem = pl.BlockSpec(memory_space=pltpu.VMEM)
        dma = pltpu.SemaphoreType.DMA
        big, small = jax.ShapeDtypeStruct((rows, width), BF16), jax.ShapeDtypeStruct((1, width), F32)
        products = 6 * rows * rows + 6 * rows * HEAD_DIM
        results = pl.pallas_call(
            functools.partial(kernel, n, g, fs, chunks, groups),
            out_shape=(big, big, big, small),
            in_specs=[any_space] * 4 + [vmem],
            out_specs=(any_space, any_space, any_space, vmem),
            scratch_shapes=[pltpu.VMEM((rows, width), BF16)] * 5
            + [pltpu.VMEM((rows, width), F32)] * 3
            + [pltpu.VMEM((rows, width), BF16)] * 3
            + [
                pltpu.VMEM((2, state, HEAD_DIM), F32),
                pltpu.VMEM((2, g, piece, HEAD_DIM), F32),
                pltpu.VMEM((2, piece, HEAD_DIM), F32),
                pltpu.VMEM((2, piece, HEAD_DIM), F32),
                pltpu.VMEM((2, g, piece, HEAD_DIM), F32),
                pltpu.VMEM((2, state, HEAD_DIM), F32),
                pltpu.VMEM((rows, HEAD_DIM), F32),
                pltpu.VMEM((rows, HEAD_DIM), F32),
                pltpu.VMEM((fs, rows, HEAD_DIM), F32),
                pltpu.VMEM((g, 1, width), F32),
                pltpu.VMEM((m, 1, width), F32),
                dma((4,)),
                dma((3, heads)),
                dma((2, g, chunks)),
                dma((2, g, chunks)),
                dma((2, chunks)),
                dma((2, chunks)),
                dma((2, g, chunks)),
                dma((2, g, chunks)),
                dma((fs,)),
                dma((fs,)),
                dma((g,)),
                dma((g,)),
                dma((m,)),
                dma((m,)),
            ],
            compiler_params=pltpu.CompilerParams(
                collective_id=0, has_side_effects=True, vmem_limit_bytes=56 * 2**20
            ),
            cost_estimate=pl.CostEstimate(
                flops=2 * products * width, bytes_accessed=14 * rows * width, transcendentals=rows
            ),
        )(query, key, value, cotangent, gain.reshape(1, width))
        return results[0], results[1], results[2], results[3].reshape(width)

    in_specs = (P("seq", "fsdp"), P("seq", "fsdp"), P("seq", "fsdp"), P("seq", "fsdp"), P("fsdp"))
    out_specs = (P("seq", "fsdp"), P("seq", "fsdp"), P("seq", "fsdp"), P("fsdp"))
    return jax.shard_map(shards, mesh=mesh, in_specs=in_specs, out_specs=out_specs, check_vma=False)
```

time: 515 us -> 81.9 us (0.16)
  waiting for transfers between devices: 306 us -> 0 us
  Pallas kernels: 0 us -> 73.4 us
  blocking collectives: 69.3 us -> 0 us
  matrix products: 56.4 us -> 0 us
  other arithmetic: 32.1 us -> 0 us
  local copies, waits for them, and re-layouts: 35 us -> 7.58 us
  between operations: 14.2 us -> 0.65 us
    all_gather x2 -> x0, waiting for transfers between devices: 306 us -> none  [prefix_2(): gathered = lax.all_gather(part, axis)]
    pallas_call x0 -> x1, Pallas kernels: none -> 73.4 us  [shards(): pl.pallas_call(functools.partial(kernel, n, g, fs, chunks, groups), out_s...]
    psum x3 -> x0, blocking collectives: 69.3 us -> none  [the longest x1 64.2 us: shards(): total_gain = lax.psum(partial_gain, 'seq')]
    dot_general x12 -> x0, matrix products: 56.4 us -> none  [the longest x1 7.35 us: shards(): jnp.einsum('hts,tha->sha', score_grad, queries, preferred_element_type=jn...]
    add x15 -> x0, other arithmetic: 22.3 us -> none  [add_states(): return earlier + later]
    reshape x3 -> x0, local copies, waits for them, and re-layouts: 13.6 us -> none  [the longest x1 5.44 us: shards(): attended = attended.reshape(rows, width)]
    unnamed x22 -> x10, local copies, waits for them, and re-layouts: 18.7 us -> 7.58 us
  transfers between devices with their start and end apart: 2 -> 0, of which waited for: 2 -> 0; matrix products, arithmetic and copies ran while one was open for 7% -> 0% of each run, Pallas kernels for 0% -> 0%
where the time goes in v1:
time: 81.9 us; the launch traced here: 81.7 us
  Pallas kernels  73.4 us (90%)
  local copies, waits for them, and re-layouts  7.58 us (9%)
    pallas_call x1, Pallas kernels, shards(): pl.pallas_call(functools.partial(kernel, n, g, fs, chunks, groups), out_s...  73.4 us
    unnamed x10, local copies, waits for them, and re-layouts  7.58 us

profile of v1, /device:TPU:0, one launch (start us, length us, event | category | flops | bytes accessed | tf_op | source)
XLA Modules:
  0.0 81.7 jit_solution(14253427045488287740)
XLA Ops:
  0.6 73.4 %shard_map.84 = (bf16[512,2048]{1,0:T(8,128)(2,1)}, bf16[512,2048]{1,0:T(8,128)(2,1)}, bf16[512,2048]{1,0:T(8,128)(2,1)}, f32[1,2048]{1,0:T(1,128)}) custom-call(bf16[512,2048]{1,0:T(8,128)(2,1)} %q_hbm.1, bf16[512,2048]{1,0:T(8,128)(2,1)} %k_hbm.1, bf16[512,2048]{1,0:T(8,128)(2,1)} %v_hbm.1, bf16[512,2048]{1,0:T(8,128)(2,1)} %c_hbm.1, f32[1,2048]{1,0:T(1,128)} %bitcast.3), custom_call_target="tpu_custom_call" | custom-call | flops 8053063680 | bytes 14680064 | tf_op jit(solution)/shard_map/pallas_call | solution.py:437
  74.1 0.0 copy-start.1
  74.1 3.3 %copy.13 = bf16[512,2048]{1,0:T(8,128)(2,1)} copy(bf16[512,2048]{1,0:T(8,128)(2,1)} %get-tuple-element.16) | data formatting | bytes 4194304
  77.4 0.0 copy-done.1
  77.4 0.0 copy-start
  77.4 1.3 %copy.14 = bf16[512,2048]{1,0:T(8,128)(2,1)} copy(bf16[512,2048]{1,0:T(8,128)(2,1)S(1)} %copy-done.1) | data formatting | bytes 4194304
  78.7 1.0 %copy-done = bf16[512,2048]{1,0:T(8,128)(2,1)S(1)} copy-done((bf16[512,2048]{1,0:T(8,128)(2,1)S(1)}, bf16[512,2048]{1,0:T(8,128)(2,1)}, u32[]{:S(2)}) %copy-start) | copy-done | bytes 2097176
  79.7 0.0 copy-start.2
  79.7 1.3 %copy.15 = bf16[512,2048]{1,0:T(8,128)(2,1)} copy(bf16[512,2048]{1,0:T(8,128)(2,1)S(1)} %copy-done) | data formatting | bytes 4194304
  81.1 0.0 copy-done.2
  81.1 0.6 copy.16
Async XLA Ops:
  74.1 3.3 %copy-start.1 = (bf16[512,2048]{1,0:T(8,128)(2,1)S(1)}, bf16[512,2048]{1,0:T(8,128)(2,1)}, u32[]{:S(2)}) copy-start(bf16[512,2048]{1,0:T(8,128)(2,1)} %get-tuple-element.17) | copy-start | bytes 6291460
  77.4 2.3 %copy-start = (bf16[512,2048]{1,0:T(8,128)(2,1)S(1)}, bf16[512,2048]{1,0:T(8,128)(2,1)}, u32[]{:S(2)}) copy-start(bf16[512,2048]{1,0:T(8,128)(2,1)} %get-tuple-element.18) | copy-start | bytes 6291460
  79.7 1.3 %copy-start.2 = (f32[1,2048]{1,0:T(1,128)S(1)}, f32[1,2048]{1,0:T(1,128)}, u32[]{:S(2)}) copy-start(f32[1,2048]{1,0:T(1,128)} %get-tuple-element.11) | copy-start | bytes 24580

commit v2 on v1

--- a/solution.py
+++ b/solution.py
@@ -54,7 +54,7 @@
 class Scan:
     def __init__(self, which, reverse, g, m, chunks, refs, sems):
         self.which, self.reverse, self.g, self.m, self.chunks = which, reverse, g, m, chunks
-        self.own, self.slots, self.carry, self.fwd, self.outs, self.result = refs
+        self.own, self.slots, self.carry, self.fwd, self.before, self.outs, self.result = refs
         self.a_send, self.a_recv, self.z_send, self.z_recv, self.b_send, self.b_recv = sems
         me = lax.axis_index("seq")
         self.z, self.i = me // g, lax.rem(me, g)
@@ -82,17 +82,36 @@
             device_id_type=MESH,
         )
 
-    def chain(self, j):
-        nearer = self.z - 1 if self.reverse else self.z + 1
-        target = jnp.clip(nearer, 0, self.m - 1)
+    def place(self):
+        return self.m - 1 - self.z if self.reverse else self.z
+
+    def chain(self, level, t, j):
+        place = jnp.clip(self.place() + 1 + t, 0, self.m - 1)
+        group = self.m - 1 - place if self.reverse else place
         return pltpu.make_async_remote_copy(
-            src_ref=self.fwd.at[self.part(j)],
-            dst_ref=self.carry.at[self.part(j)],
-            send_sem=self.z_send.at[self.which, j],
-            recv_sem=self.z_recv.at[self.which, j],
-            device_id={"seq": target * self.g + self.i},
+            src_ref=self.fwd.at[level, self.part(j)],
+            dst_ref=self.carry.at[level, self.part(j)],
+            send_sem=self.z_send.at[self.which, level, t, j],
+            recv_sem=self.z_recv.at[self.which, level, j],
+            device_id={"seq": group * self.g + self.i},
             device_id_type=MESH,
         )
+
+    def levels(self):
+        return range(self.m.bit_length() - 1)
+
+    def sends(self, level):
+        return lax.rem(self.place(), 2 << level) == (1 << level) - 1
+
+    def receives(self, level):
+        return lax.rem(self.place(), 2 << level) >= 1 << level
+
+    def forward(self, level, j, value):
+        @pl.when(self.sends(level))
+        def _():
+            self.fwd[level, self.part(j)] = value()
+            for t in range(1 << level):
+                self.chain(level, t, j).start()
 
     def hand(self, d, j, arriving=False):
         p = self.peer(d)
@@ -106,34 +125,31 @@
             device_id_type=MESH,
         )
 
-    def first(self):
-        return self.z == (self.m - 1 if self.reverse else 0)
-
-    def last(self):
-        return self.z == (0 if self.reverse else self.m - 1)
+    def total(self, j):
+        total = self.slots[0, self.part(j)]
+        for p in range(1, self.g):
+            total = total + self.slots[p, self.part(j)]
+        return total
+
+    def gather(self, j):
+        for d in range(1, self.g):
+            self.spread(d, j, True).wait_recv()
+        if self.m > 1:
+            self.forward(0, j, lambda: self.total(j))
 
     def process(self, j):
         part = self.part(j)
-        for d in range(1, self.g):
-            self.spread(d, j, True).wait_recv()
-        total = self.slots[0, part]
-        for p in range(1, self.g):
-            total = total + self.slots[p, part]
-
-        @pl.when(self.first())
-        def _():
-            self.carry[part] = jnp.zeros_like(total)
-
-        @pl.when(jnp.logical_not(self.first()))
-        def _():
-            self.chain(j).wait_recv()
-
-        @pl.when(jnp.logical_not(self.last()))
-        def _():
-            self.fwd[part] = self.carry[part] + total
-            self.chain(j).start()
-
-        running = self.carry[part]
+        self.before[part] = jnp.zeros((self.ch, HEAD_DIM), F32)
+        for level in self.levels():
+            if level:
+                self.forward(level, j, lambda: self.before[part] + self.total(j))
+
+            @pl.when(self.receives(level))
+            def _():
+                self.chain(level, 0, j).wait_recv()
+                self.before[part] += self.carry[level, part]
+
+        running = self.before[part]
         order = range(self.g)
         for p in reversed(order) if self.reverse else order:
             self.outs[p, part] = running
@@ -148,19 +164,22 @@
                 self.spread(d, j).wait_send()
                 self.hand(d, j).wait_send()
 
-            @pl.when(jnp.logical_not(self.last()))
-            def _():
-                self.chain(j).wait_send()
+            for level in self.levels():
+
+                @pl.when(self.sends(level))
+                def _():
+                    for t in range(1 << level):
+                        self.chain(level, t, j).wait_send()
 
 
 def kernel(
-    n, g, fs, chunks, groups,
+    n, g, fs, chunks,
     q_hbm, k_hbm, v_hbm, c_hbm, gain_ref,
-    qg_hbm, kg_hbm, vg_hbm, gg_ref,
-    q, k, v, cot, do, att, kg_l, vg_l, qg, kg, vg,
-    own, slots, carry, fwd, outs, result,
+    qg, kg, vg, gg_ref,
+    q, k, v, cot, do, att, kg_l, vg_l, w_top, w_low,
+    own, slots, carry, fwd, before, outs, result,
     sq, cr, stats, gp, gz,
-    in_sem, out_sem, a_send, a_recv, z_send, z_recv, b_send, b_recv,
+    in_sem, a_send, a_recv, z_send, z_recv, b_send, b_recv,
     f_send, f_recv, g_send, g_recv, h_send, h_recv,
 ):
     rows, width = q.shape
@@ -194,7 +213,7 @@
 
     sems = (a_send, a_recv, z_send, z_recv, b_send, b_recv)
     scans = [
-        Scan(w, w == 1, g, m, chunks, tuple(r.at[w] for r in (own, slots, carry, fwd, outs, result)), sems)
+        Scan(w, w == 1, g, m, chunks, tuple(r.at[w] for r in (own, slots, carry, fwd, before, outs, result)), sems)
         for w in range(2)
     ]
     per = heads // g
@@ -259,12 +278,23 @@
         w1 = lower(dot_abt(q[low, cols], kh), half)
         att[top, cols] = dot_ab(w0, v[top, cols])
         att[low, cols] = dot_ab(w1, vh)
+        w_top[head] = upper(dot_abt(k[top, cols], q[:, cols]))
+        w_low[head] = upper(dot_abt(k[low, cols], q[low, cols]))
         return 0
 
-    for j in range(chunks):
-        lax.fori_loop(groups[j], groups[j + 1], inside, 0)
-        scans[0].process(j)
-    lax.fori_loop(groups[chunks], heads, inside, 0)
+    def beside(scan, unit, ahead, between):
+        done = 0
+        for j in range(chunks):
+            for count, step in ((ahead if j else between, scan.gather), (between, scan.process)):
+                upto = min(done + count, heads)
+                if upto > done:
+                    lax.fori_loop(done, upto, unit, 0)
+                done = upto
+                step(j)
+        if heads > done:
+            lax.fori_loop(done, heads, unit, 0)
+
+    beside(scans[0], inside, 2, 1)
     loads[3].wait()
 
     sq[...] = jnp.zeros_like(sq)
@@ -355,18 +385,11 @@
         t1 = upper(dot_abt(v[low, cols], d1))
         kg_l[top, cols] = dot_ab(t0, qh)
         kg_l[low, cols] = dot_ab(t1, q1)
-        w0 = upper(dot_abt(k0, qh))
-        w1 = upper(dot_abt(k[low, cols], q1))
-        vg_l[top, cols] = dot_ab(w0, dh)
-        vg_l[low, cols] = dot_ab(w1, d1)
+        vg_l[top, cols] = dot_ab(w_top[head], dh)
+        vg_l[low, cols] = dot_ab(w_low[head], d1)
         return 0
 
-    for j in range(chunks):
-        lax.fori_loop(groups[j], groups[j + 1], backward, 0)
-        scans[1].process(j)
-    lax.fori_loop(groups[chunks], heads, backward, 0)
-    store_q = pltpu.make_async_copy(qg, qg_hbm, out_sem.at[0, 0])
-    store_q.start()
+    beside(scans[1], backward, 1, 1)
 
     for d in range(1, g):
         gain_near(d, lax.rem(i + d, g)).wait_recv()
@@ -377,17 +400,11 @@
     for d in range(1, m):
         gain_far(d, z).start()
 
-    def store(at, src, dst, head):
-        cols = cols_of(head)
-        return pltpu.make_async_copy(src.at[:, cols], dst.at[:, cols], out_sem.at[at, head])
-
     def last(head):
         cols = cols_of(head)
         suffix = state_at(scans[1], head)
         kg[:, cols] = (kg_l[:, cols] + dot_abt(v[:, cols], suffix)).astype(BF16)
         vg[:, cols] = (vg_l[:, cols] + dot_ab(k[:, cols], suffix)).astype(BF16)
-        store(1, kg, kg_hbm, head).start()
-        store(2, vg, vg_hbm, head).start()
 
     arrivals(scans[1], last)
 
@@ -406,14 +423,17 @@
         gain_near(d, i).wait_send()
     for d in range(1, m):
         gain_far(d, z).wait_send()
-    store_q.wait()
-
-    def stored(head, _):
-        store(1, kg, kg_hbm, head).wait()
-        store(2, vg, vg_hbm, head).wait()
-        return 0
-
-    lax.fori_loop(0, heads, stored, 0)
+
+
+def store(qg, kg, vg, gg, qg_hbm, kg_hbm, vg_hbm, gg_hbm, sem):
+    copies = [
+        pltpu.make_async_copy(src, dst, sem.at[at])
+        for at, (src, dst) in enumerate(((qg, qg_hbm), (kg, kg_hbm), (vg, vg_hbm), (gg, gg_hbm)))
+    ]
+    for copy in copies:
+        copy.start()
+    for copy in copies:
+        copy.wait()
 
 
 def solution(mesh):
@@ -427,25 +447,27 @@
         chunks = max(heads // g, 1)
         state = heads * HEAD_DIM
         piece = state // g
-        step = heads // (chunks + 1)
-        groups = tuple(min(heads, (j * heads) // (chunks + 1)) for j in range(chunks + 1))
+        levels = max(m.bit_length() - 1, 1)
         any_space = pl.BlockSpec(memory_space=pl.ANY)
         vmem = pl.BlockSpec(memory_space=pltpu.VMEM)
         dma = pltpu.SemaphoreType.DMA
         big, small = jax.ShapeDtypeStruct((rows, width), BF16), jax.ShapeDtypeStruct((1, width), F32)
+        held = pltpu.VMEM((rows, width), BF16)
         products = 6 * rows * rows + 6 * rows * HEAD_DIM
         results = pl.pallas_call(
-            functools.partial(kernel, n, g, fs, chunks, groups),
-            out_shape=(big, big, big, small),
+            functools.partial(kernel, n, g, fs, chunks),
+            out_shape=(held, held, held, pltpu.VMEM((1, width), F32)),
             in_specs=[any_space] * 4 + [vmem],
-            out_specs=(any_space, any_space, any_space, vmem),
+            out_specs=(vmem, vmem, vmem, vmem),
             scratch_shapes=[pltpu.VMEM((rows, width), BF16)] * 5
             + [pltpu.VMEM((rows, width), F32)] * 3
-            + [pltpu.VMEM((rows, width), BF16)] * 3
             + [
+                pltpu.VMEM((heads, rows // 2, rows), BF16),
+                pltpu.VMEM((heads, rows // 2, rows // 2), BF16),
                 pltpu.VMEM((2, state, HEAD_DIM), F32),
                 pltpu.VMEM((2, g, piece, HEAD_DIM), F32),
-                pltpu.VMEM((2, piece, HEAD_DIM), F32),
+                pltpu.VMEM((2, levels, piece, HEAD_DIM), F32),
+                pltpu.VMEM((2, levels, piece, HEAD_DIM), F32),
                 pltpu.VMEM((2, piece, HEAD_DIM), F32),
                 pltpu.VMEM((2, g, piece, HEAD_DIM), F32),
                 pltpu.VMEM((2, state, HEAD_DIM), F32),
@@ -455,11 +477,10 @@
                 pltpu.VMEM((g, 1, width), F32),
                 pltpu.VMEM((m, 1, width), F32),
                 dma((4,)),
-                dma((3, heads)),
                 dma((2, g, chunks)),
                 dma((2, g, chunks)),
-                dma((2, chunks)),
-                dma((2, chunks)),
+                dma((2, levels, max(m // 2, 1), chunks)),
+                dma((2, levels, chunks)),
                 dma((2, g, chunks)),
                 dma((2, g, chunks)),
                 dma((fs,)),
@@ -470,13 +491,20 @@
                 dma((m,)),
             ],
             compiler_params=pltpu.CompilerParams(
-                collective_id=0, has_side_effects=True, vmem_limit_bytes=56 * 2**20
+                collective_id=0, has_side_effects=True, vmem_limit_bytes=50 * 2**20
             ),
             cost_estimate=pl.CostEstimate(
                 flops=2 * products * width, bytes_accessed=14 * rows * width, transcendentals=rows
             ),
         )(query, key, value, cotangent, gain.reshape(1, width))
-        return results[0], results[1], results[2], results[3].reshape(width)
+        grads = pl.pallas_call(
+            store,
+            out_shape=(big, big, big, small),
+            in_specs=[any_space] * 4,
+            out_specs=(any_space,) * 4,
+            scratch_shapes=[dma((4,))],
+        )(*results)
+        return (*grads[:3], grads[3].reshape(width))
 
     in_specs = (P("seq", "fsdp"), P("seq", "fsdp"), P("seq", "fsdp"), P("seq", "fsdp"), P("fsdp"))
     out_specs = (P("seq", "fsdp"), P("seq", "fsdp"), P("seq", "fsdp"), P("fsdp"))

time: 81.9 us -> 270 us (3.30)
  Pallas kernels: 73.4 us -> 265 us
  local copies, waits for them, and re-layouts: 7.58 us -> 4.55 us
    pallas_call x1 -> x2, Pallas kernels: 73.4 us -> 265 us  [the longest x1 192 us: shards(): pl.pallas_call(store, out_shape=(big, big, big, small), in_specs=[any_spa...]
    unnamed x10 -> x8, local copies, waits for them, and re-layouts: 7.58 us -> 4.55 us
where the time goes in v2:
time: 270 us
  Pallas kernels  265 us (98%)
  local copies, waits for them, and re-layouts  4.55 us (2%)
    pallas_call x1, Pallas kernels, shards(): pl.pallas_call(store, out_shape=(big, big, big, small), in_specs=[any_spa...  192 us
    pallas_call x1, Pallas kernels, shards(): pl.pallas_call(functools.partial(kernel, n, g, fs, chunks), out_shape=(he...  72.8 us

profile of v2, /device:TPU:0, one launch (start us, length us, event | category | flops | bytes accessed | tf_op | source)
XLA Modules:
  0.0 270.1 jit_solution(2198179398066126782)
XLA Ops:
  0.6 72.8 %shard_map.84 = (bf16[512,2048]{1,0:T(8,128)(2,1)S(1)}, bf16[512,2048]{1,0:T(8,128)(2,1)S(1)}, bf16[512,2048]{1,0:T(8,128)(2,1)S(1)}, f32[1,2048]{1,0:T(1,128)S(1)}) custom-call(bf16[512,2048]{1,0:T(8,128)(2,1)} %q_hbm.1, bf16[512,2048]{1,0:T(8,128)(2,1)} %k_hbm.1, bf16[512,2048]{1,0:T(8,128)(2,1)} %v_hbm.1, bf16[512,2048]{1,0:T(8,128)(2,1)} %c_hbm.1, ...), custom_call_target="tpu_custom_call" | custom-call | flops 8053063680 | bytes 14680064 | tf_op jit(solution)/shard_map/pallas_call | solution.py:457
  73.4 0.0 copy-start
  73.4 1.3 copy-done
  74.8 0.0 copy-start.1
  74.8 1.3 copy-done.1
  76.1 0.0 copy-start.2
  76.1 1.3 copy-done.2
  77.4 0.0 copy-start.3
  77.4 0.6 copy-done.3
  78.0 192.0 %shard_map.85 = (bf16[512,2048]{1,0:T(8,128)(2,1)}, bf16[512,2048]{1,0:T(8,128)(2,1)}, bf16[512,2048]{1,0:T(8,128)(2,1)}, f32[1,2048]{1,0:T(1,128)}) custom-call(bf16[512,2048]{1,0:T(8,128)(2,1)} %copy-done, bf16[512,2048]{1,0:T(8,128)(2,1)} %copy-done.1, bf16[512,2048]{1,0:T(8,128)(2,1)} %copy-done.2, f32[1,2048]{1,0:T(1,128)} %copy-done.3), custom_call_target="tpu_custom_call" | custom-call | tf_op jit(solution)/shard_map/pallas_call | solution.py:500
Async XLA Ops:
  73.4 1.3 copy-start
  74.8 1.3 copy-start.1
  76.1 1.3 copy-start.2
  77.4 0.6 copy-start.3

commit v3 on v2

--- a/solution.py
+++ b/solution.py
@@ -68,7 +68,7 @@
         return pl.ds(pl.multiple_of(p * self.piece + j * self.ch, self.ch), self.ch)
 
     def part(self, j):
-        return pl.ds(j * self.ch, self.ch)
+        return pl.ds(pl.multiple_of(j * self.ch, self.ch), self.ch)
 
     def spread(self, d, j, arriving=False):
         p = self.peer(d)
@@ -159,17 +159,20 @@
         self.result[self.rows(self.i, j)] = self.outs[self.i, part]
 
     def drain(self):
-        for j in range(self.chunks):
+        def turn(j, _):
             for d in range(1, self.g):
                 self.spread(d, j).wait_send()
                 self.hand(d, j).wait_send()
-
             for level in self.levels():
 
                 @pl.when(self.sends(level))
                 def _():
                     for t in range(1 << level):
                         self.chain(level, t, j).wait_send()
+
+            return 0
+
+        lax.fori_loop(0, self.chunks, turn, 0)
 
 
 def kernel(
@@ -218,25 +221,25 @@
     ]
     per = heads // g
 
-    def head_order(turn):
+    def make_states(scan, state_of):
+        def turn(t, _):
+            j, d = t // g, lax.rem(t + 1, g)
+            p = scan.peer(d)
+            state = state_of(p * per + j)
+            scan.own[scan.rows(p, j)] = state
+
+            @pl.when(d == 0)
+            def _():
+                scan.slots[i, scan.part(j)] = state
+
+            @pl.when(d != 0)
+            def _():
+                scan.spread(d, j).start()
+
+            return 0
+
         if per:
-            for j in range(chunks):
-                for d in range(g):
-                    turn(lax.rem(i + d, g) * per + j, d, j)
-
-    def make_states(scan, state_of):
-        def turn(head, d, j):
-            state = state_of(head)
-            if d == 0:
-                scan.slots[i, scan.part(j)] = state
-            else:
-                scan.own[scan.rows(scan.peer(d), j)] = state
-                scan.spread(d, j).start()
-
-        if per:
-            for j in range(chunks):
-                for d in list(range(1, g)) + [0]:
-                    turn(lax.rem(i + d, g) * per + j, d, j)
+            lax.fori_loop(0, chunks * g, turn, 0)
         else:
             for head in range(heads):
                 scan.own[pl.ds(head * HEAD_DIM, HEAD_DIM)] = state_of(head)
@@ -246,12 +249,18 @@
                     scan.spread(d, j).start()
 
     def arrivals(scan, visit):
+        def turn(t, _):
+            j, d = t // g, lax.rem(t, g)
+
+            @pl.when(d != 0)
+            def _():
+                scan.hand(d, j, True).wait_recv()
+
+            visit(scan.peer(d) * per + j)
+            return 0
+
         if per:
-            for j in range(chunks):
-                for d in range(g):
-                    if d:
-                        scan.hand(d, j, True).wait_recv()
-                    visit(lax.rem(i + d, g) * per + j)
+            lax.fori_loop(0, chunks * g, turn, 0)
         else:
             for j in range(chunks):
                 for d in range(1, g):
@@ -271,7 +280,7 @@
 
     top, low = pl.ds(0, half), pl.ds(half, half)
 
-    def inside(head, _):
+    def inside(head):
         cols = cols_of(head)
         kh, vh = k[:, cols], v[:, cols]
         w0 = lower(dot_abt(q[top, cols], k[top, cols]), 0)
@@ -280,19 +289,32 @@
         att[low, cols] = dot_ab(w1, vh)
         w_top[head] = upper(dot_abt(k[top, cols], q[:, cols]))
         w_low[head] = upper(dot_abt(k[low, cols], q[low, cols]))
-        return 0
 
     def beside(scan, unit, ahead, between):
-        done = 0
-        for j in range(chunks):
-            for count, step in ((ahead if j else between, scan.gather), (between, scan.process)):
-                upto = min(done + count, heads)
-                if upto > done:
-                    lax.fori_loop(done, upto, unit, 0)
-                done = upto
-                step(j)
-        if heads > done:
-            lax.fori_loop(done, heads, unit, 0)
+        step = ahead + between
+
+        def turn(u, _):
+            unit(u)
+            j = u // step
+
+            @pl.when(jnp.logical_and(lax.rem(u, step) == ahead - 1, j < chunks))
+            def _():
+                scan.gather(j)
+
+            @pl.when(jnp.logical_and(lax.rem(u, step) == step - 1, j < chunks))
+            def _():
+                scan.process(j)
+
+            return 0
+
+        if heads >= step * chunks:
+            lax.fori_loop(0, heads, turn, 0)
+        else:
+            for head in range(heads):
+                unit(head)
+            for j in range(chunks):
+                scan.gather(j)
+                scan.process(j)
 
     beside(scans[0], inside, 2, 1)
     loads[3].wait()
@@ -372,7 +394,7 @@
     for d in range(1, g):
         gain_near(d, i).start()
 
-    def backward(head, _):
+    def backward(head):
         cols = cols_of(head)
         qh, kh, vh, dh = q[:, cols], k[:, cols], v[:, cols], do[:, cols]
         q1, k0, v0, d1 = q[low, cols], k[top, cols], v[top, cols], do[low, cols]
@@ -387,7 +409,6 @@
         kg_l[low, cols] = dot_ab(t1, q1)
         vg_l[top, cols] = dot_ab(w_top[head], dh)
         vg_l[low, cols] = dot_ab(w_low[head], d1)
-        return 0
 
     beside(scans[1], backward, 1, 1)
 
@@ -503,6 +524,7 @@
             in_specs=[any_space] * 4,
             out_specs=(any_space,) * 4,
             scratch_shapes=[dma((4,))],
+            compiler_params=pltpu.CompilerParams(vmem_limit_bytes=2**20),
         )(*results)
         return (*grads[:3], grads[3].reshape(width))
 

time: 270 us -> 77 us (0.29)
  Pallas kernels: 265 us -> 76.1 us
  local copies, waits for them, and re-layouts: 4.55 us -> 0 us
    pallas_call x1, Pallas kernels: 192 us -> 2.74 us  [shards(): pl.pallas_call(store, out_shape=(big, big, big, small), in_specs=[any_spa...]
    unnamed x8 -> x0, local copies, waits for them, and re-layouts: 4.55 us -> none
where the time goes in v3:
time: 77 us; the launch traced here: 76.8 us
  Pallas kernels  76.1 us (99%)
    pallas_call x1, Pallas kernels, shards(): pl.pallas_call(functools.partial(kernel, n, g, fs, chunks), out_shape=(he...  73.4 us
    pallas_call x1, Pallas kernels, shards(): pl.pallas_call(store, out_shape=(big, big, big, small), in_specs=[any_spa...  2.74 us

profile of v3, /device:TPU:0, one launch (start us, length us, event | category | flops | bytes accessed | tf_op | source)
XLA Modules:
  0.0 76.8 jit_solution(14968590869662189518)
XLA Ops:
  0.6 73.4 %shard_map.84 = (bf16[512,2048]{1,0:T(8,128)(2,1)S(1)}, bf16[512,2048]{1,0:T(8,128)(2,1)S(1)}, bf16[512,2048]{1,0:T(8,128)(2,1)S(1)}, f32[1,2048]{1,0:T(1,128)S(1)}) custom-call(bf16[512,2048]{1,0:T(8,128)(2,1)} %q_hbm.1, bf16[512,2048]{1,0:T(8,128)(2,1)} %k_hbm.1, bf16[512,2048]{1,0:T(8,128)(2,1)} %v_hbm.1, bf16[512,2048]{1,0:T(8,128)(2,1)} %c_hbm.1, ...), custom_call_target="tpu_custom_call" | custom-call | flops 8053063680 | bytes 14680064 | tf_op jit(solution)/shard_map/pallas_call | solution.py:478
  74.0 2.7 %shard_map.85 = (bf16[512,2048]{1,0:T(8,128)(2,1)}, bf16[512,2048]{1,0:T(8,128)(2,1)}, bf16[512,2048]{1,0:T(8,128)(2,1)}, f32[1,2048]{1,0:T(1,128)}) custom-call(bf16[512,2048]{1,0:T(8,128)(2,1)S(1)} %get-tuple-element.12.qg, bf16[512,2048]{1,0:T(8,128)(2,1)S(1)} %get-tuple-element.13.kg, bf16[512,2048]{1,0:T(8,128)(2,1)S(1)} %get-tuple-element.14.vg, ...), custom_call_target="tpu_custom_call" | custom-call | tf_op jit(solution)/shard_map/pallas_call | solution.py:521

commit v4 on v3

--- a/solution.py
+++ b/solution.py
@@ -35,8 +35,8 @@
     return size
 
 
-def lower(block, offset):
-    row = lax.broadcasted_iota(jnp.int32, block.shape, 0) + offset
+def lower(block):
+    row = lax.broadcasted_iota(jnp.int32, block.shape, 0)
     col = lax.broadcasted_iota(jnp.int32, block.shape, 1)
     return jnp.where(row >= col, block, 0.0).astype(BF16)
 
@@ -49,6 +49,14 @@
 
 def cols_of(head):
     return pl.ds(pl.multiple_of(head * HEAD_DIM, HEAD_DIM), HEAD_DIM)
+
+
+def bottom(left, right):
+    return jnp.concatenate([left.astype(BF16), lower(right)], axis=1)
+
+
+def top_of(left, right):
+    return jnp.concatenate([upper(left), right.astype(BF16)], axis=1)
 
 
 class Scan:
@@ -282,33 +290,29 @@
 
     def inside(head):
         cols = cols_of(head)
-        kh, vh = k[:, cols], v[:, cols]
-        w0 = lower(dot_abt(q[top, cols], k[top, cols]), 0)
-        w1 = lower(dot_abt(q[low, cols], kh), half)
+        vh = v[:, cols]
+        q0, q1, k0, k1 = q[top, cols], q[low, cols], k[top, cols], k[low, cols]
+        w0 = lower(dot_abt(q0, k0))
+        w1 = bottom(dot_abt(q1, k0), dot_abt(q1, k1))
         att[top, cols] = dot_ab(w0, v[top, cols])
         att[low, cols] = dot_ab(w1, vh)
-        w_top[head] = upper(dot_abt(k[top, cols], q[:, cols]))
-        w_low[head] = upper(dot_abt(k[low, cols], q[low, cols]))
-
-    def beside(scan, unit, ahead, between):
-        step = ahead + between
-
+        w_top[head] = top_of(dot_abt(k0, q0), dot_abt(k0, q1))
+        w_low[head] = upper(dot_abt(k1, q1))
+
+    def beside(scan, unit, width):
         def turn(u, _):
-            unit(u)
-            j = u // step
-
-            @pl.when(jnp.logical_and(lax.rem(u, step) == ahead - 1, j < chunks))
+            for at in range(width):
+                unit(u * width + at)
+
+            @pl.when(u < chunks)
             def _():
-                scan.gather(j)
-
-            @pl.when(jnp.logical_and(lax.rem(u, step) == step - 1, j < chunks))
-            def _():
-                scan.process(j)
+                scan.gather(u)
+                scan.process(u)
 
             return 0
 
-        if heads >= step * chunks:
-            lax.fori_loop(0, heads, turn, 0)
+        if heads >= width * chunks and heads % width == 0:
+            lax.fori_loop(0, heads // width, turn, 0)
         else:
             for head in range(heads):
                 unit(head)
@@ -316,7 +320,7 @@
                 scan.gather(j)
                 scan.process(j)
 
-    beside(scans[0], inside, 2, 1)
+    beside(scans[0], inside, 2)
     loads[3].wait()
 
     sq[...] = jnp.zeros_like(sq)
@@ -396,21 +400,22 @@
 
     def backward(head):
         cols = cols_of(head)
-        qh, kh, vh, dh = q[:, cols], k[:, cols], v[:, cols], do[:, cols]
-        q1, k0, v0, d1 = q[low, cols], k[top, cols], v[top, cols], do[low, cols]
+        qh, kh, dh = q[:, cols], k[:, cols], do[:, cols]
+        q1, k0, v0, v1 = q[low, cols], k[top, cols], v[top, cols], v[low, cols]
+        d0, d1 = do[top, cols], do[low, cols]
         from_prefix = dot_abt(dh, state_at(scans[0], head))
-        s0 = lower(dot_abt(do[top, cols], v0), 0)
-        s1 = lower(dot_abt(d1, vh), half)
+        s0 = lower(dot_abt(d0, v0))
+        s1 = bottom(dot_abt(d1, v0), dot_abt(d1, v1))
         qg[top, cols] = (dot_ab(s0, k0) + from_prefix[:half]).astype(BF16)
         qg[low, cols] = (dot_ab(s1, kh) + from_prefix[half:]).astype(BF16)
-        t0 = upper(dot_abt(v0, dh))
-        t1 = upper(dot_abt(v[low, cols], d1))
+        t0 = top_of(dot_abt(v0, d0), dot_abt(v0, d1))
+        t1 = upper(dot_abt(v1, d1))
         kg_l[top, cols] = dot_ab(t0, qh)
         kg_l[low, cols] = dot_ab(t1, q1)
         vg_l[top, cols] = dot_ab(w_top[head], dh)
         vg_l[low, cols] = dot_ab(w_low[head], d1)
 
-    beside(scans[1], backward, 1, 1)
+    beside(scans[1], backward, 2)
 
     for d in range(1, g):
         gain_near(d, lax.rem(i + d, g)).wait_recv()

time: 77 us -> 77.9 us (1.012)
  Pallas kernels: 76.1 us -> 77 us
    pallas_call x1, Pallas kernels: 73.4 us -> 74.3 us  [shards(): pl.pallas_call(functools.partial(kernel, n, g, fs, chunks), out_shape=(he...]
where the time goes in v4:
time: 77.9 us; the launch traced here: 77.7 us
  Pallas kernels  77 us (99%)
    pallas_call x1, Pallas kernels, shards(): pl.pallas_call(functools.partial(kernel, n, g, fs, chunks), out_shape=(he...  74.3 us
    pallas_call x1, Pallas kernels, shards(): pl.pallas_call(store, out_shape=(big, big, big, small), in_specs=[any_spa...  2.74 us

profile of v4, /device:TPU:0, one launch (start us, length us, event | category | flops | bytes accessed | tf_op | source)
XLA Modules:
  0.0 77.7 jit_solution(17012042529511862225)
XLA Ops:
  0.6 74.3 %shard_map.84 = (bf16[512,2048]{1,0:T(8,128)(2,1)S(1)}, bf16[512,2048]{1,0:T(8,128)(2,1)S(1)}, bf16[512,2048]{1,0:T(8,128)(2,1)S(1)}, f32[1,2048]{1,0:T(1,128)S(1)}) custom-call(bf16[512,2048]{1,0:T(8,128)(2,1)} %q_hbm.1, bf16[512,2048]{1,0:T(8,128)(2,1)} %k_hbm.1, bf16[512,2048]{1,0:T(8,128)(2,1)} %v_hbm.1, bf16[512,2048]{1,0:T(8,128)(2,1)} %c_hbm.1, ...), custom_call_target="tpu_custom_call" | custom-call | flops 8053063680 | bytes 14680064 | tf_op jit(solution)/shard_map/pallas_call | solution.py:483
  74.9 2.7 %shard_map.85 = (bf16[512,2048]{1,0:T(8,128)(2,1)}, bf16[512,2048]{1,0:T(8,128)(2,1)}, bf16[512,2048]{1,0:T(8,128)(2,1)}, f32[1,2048]{1,0:T(1,128)}) custom-call(bf16[512,2048]{1,0:T(8,128)(2,1)S(1)} %get-tuple-element.12.qg, bf16[512,2048]{1,0:T(8,128)(2,1)S(1)} %get-tuple-element.13.kg, bf16[512,2048]{1,0:T(8,128)(2,1)S(1)} %get-tuple-element.14.vg, ...), custom_call_target="tpu_custom_call" | custom-call | tf_op jit(solution)/shard_map/pallas_call | solution.py:526

commit v5 on v4

--- a/solution.py
+++ b/solution.py
@@ -166,10 +166,16 @@
             self.hand(d, j).start()
         self.result[self.rows(self.i, j)] = self.outs[self.i, part]
 
-    def drain(self):
+    def sent(self, j):
+        for d in range(1, self.g):
+            self.spread(d, j).wait_send()
+
+    def drain(self, unsent):
+        for j in range(self.chunks - unsent, self.chunks):
+            self.sent(j)
+
         def turn(j, _):
             for d in range(1, self.g):
-                self.spread(d, j).wait_send()
                 self.hand(d, j).wait_send()
             for level in self.levels():
 
@@ -229,7 +235,9 @@
     ]
     per = heads // g
 
-    def make_states(scan, state_of):
+    window = min(2, chunks)
+
+    def make_states(scan, state_of, first, last, send):
         def turn(t, _):
             j, d = t // g, lax.rem(t + 1, g)
             p = scan.peer(d)
@@ -240,21 +248,23 @@
             def _():
                 scan.slots[i, scan.part(j)] = state
 
-            @pl.when(d != 0)
-            def _():
+            if send:
+
+                @pl.when(d != 0)
+                def _():
+                    scan.spread(d, j).start()
+
+            return 0
+
+        lax.fori_loop(first * g, last * g, turn, 0)
+
+    def make_all(scan, state_of):
+        for head in range(heads):
+            scan.own[pl.ds(head * HEAD_DIM, HEAD_DIM)] = state_of(head)
+        for j in range(chunks):
+            scan.slots[i, scan.part(j)] = scan.own[scan.rows(i, j)]
+            for d in range(1, g):
                 scan.spread(d, j).start()
-
-            return 0
-
-        if per:
-            lax.fori_loop(0, chunks * g, turn, 0)
-        else:
-            for head in range(heads):
-                scan.own[pl.ds(head * HEAD_DIM, HEAD_DIM)] = state_of(head)
-            for j in range(chunks):
-                scan.slots[i, scan.part(j)] = scan.own[scan.rows(i, j)]
-                for d in range(1, g):
-                    scan.spread(d, j).start()
 
     def arrivals(scan, visit):
         def turn(t, _):
@@ -283,7 +293,15 @@
     loads[0].wait()
     loads[1].wait()
     pl.semaphore_wait(barrier, (g - 1) + (m - 1) + (fs - 1))
-    make_states(scans[0], lambda head: dot_atb(k[:, cols_of(head)], v[:, cols_of(head)]))
+
+    def state(head):
+        return dot_atb(k[:, cols_of(head)], v[:, cols_of(head)])
+
+    if per:
+        make_states(scans[0], state, 0, window, True)
+        make_states(scans[0], state, window, chunks, False)
+    else:
+        make_all(scans[0], state)
     loads[2].wait()
 
     top, low = pl.ds(0, half), pl.ds(half, half)
@@ -299,28 +317,36 @@
         w_top[head] = top_of(dot_abt(k0, q0), dot_abt(k0, q1))
         w_low[head] = upper(dot_abt(k1, q1))
 
-    def beside(scan, unit, width):
+    def beside(scan, unit, width, start, sends):
         def turn(u, _):
             for at in range(width):
                 unit(u * width + at)
-
-            @pl.when(u < chunks)
+            j = u + start
+            if sends:
+
+                @pl.when(j + window < chunks)
+                def _():
+                    scan.sent(j)
+                    for d in range(1, g):
+                        scan.spread(d, j + window).start()
+
+            @pl.when(j < chunks)
             def _():
-                scan.gather(u)
-                scan.process(u)
+                scan.gather(j)
+                scan.process(j)
 
             return 0
 
-        if heads >= width * chunks and heads % width == 0:
+        if per and heads % width == 0:
             lax.fori_loop(0, heads // width, turn, 0)
         else:
             for head in range(heads):
                 unit(head)
-            for j in range(chunks):
+            for j in range(start, chunks):
                 scan.gather(j)
                 scan.process(j)
 
-    beside(scans[0], inside, 2)
+    beside(scans[0], inside, 2, 0, True)
     loads[3].wait()
 
     sq[...] = jnp.zeros_like(sq)
@@ -373,7 +399,18 @@
         do[:, cols] = d_h
         return dot_atb(q[:, cols], d_h)
 
-    make_states(scans[1], grad_state)
+    def next_states(j, _):
+        scans[1].sent(j - window)
+        make_states(scans[1], grad_state, j, j + 1, True)
+        scans[1].gather(j - window)
+        scans[1].process(j - window)
+        return 0
+
+    if per:
+        make_states(scans[1], grad_state, 0, window, True)
+        lax.fori_loop(window, chunks, next_states, 0)
+    else:
+        make_all(scans[1], grad_state)
 
     def gain_near(d, slot):
         return pltpu.make_async_remote_copy(
@@ -415,7 +452,7 @@
         vg_l[top, cols] = dot_ab(w_top[head], dh)
         vg_l[low, cols] = dot_ab(w_low[head], d1)
 
-    beside(scans[1], backward, 2)
+    beside(scans[1], backward, 2, chunks - window if per else 0, False)
 
     for d in range(1, g):
         gain_near(d, lax.rem(i + d, g)).wait_recv()
@@ -442,7 +479,7 @@
     gg_ref[...] = total * (1.0 / math.sqrt(rows * n))
 
     for scan in scans:
-        scan.drain()
+        scan.drain(window)
     for d in range(1, fs):
         share(d, mine).wait_send()
     for d in range(1, g):

time: 77.9 us -> 83 us (1.065)
  Pallas kernels: 77 us -> 82.1 us
    pallas_call x1, Pallas kernels: 74.3 us -> 79.4 us  [shards(): pl.pallas_call(functools.partial(kernel, n, g, fs, chunks), out_shape=(he...]
where the time goes in v5:
time: 83 us; the launch traced here: 82.8 us
  Pallas kernels  82.1 us (99%)
    pallas_call x1, Pallas kernels, shards(): pl.pallas_call(functools.partial(kernel, n, g, fs, chunks), out_shape=(he...  79.4 us
    pallas_call x1, Pallas kernels, shards(): pl.pallas_call(store, out_shape=(big, big, big, small), in_specs=[any_spa...  2.74 us

profile of v5, /device:TPU:0, one launch (start us, length us, event | category | flops | bytes accessed | tf_op | source)
XLA Modules:
  0.0 82.8 jit_solution(646932783087780314)
XLA Ops:
  0.6 79.4 %shard_map.84 = (bf16[512,2048]{1,0:T(8,128)(2,1)S(1)}, bf16[512,2048]{1,0:T(8,128)(2,1)S(1)}, bf16[512,2048]{1,0:T(8,128)(2,1)S(1)}, f32[1,2048]{1,0:T(1,128)S(1)}) custom-call(bf16[512,2048]{1,0:T(8,128)(2,1)} %q_hbm.1, bf16[512,2048]{1,0:T(8,128)(2,1)} %k_hbm.1, bf16[512,2048]{1,0:T(8,128)(2,1)} %v_hbm.1, bf16[512,2048]{1,0:T(8,128)(2,1)} %c_hbm.1, ...), custom_call_target="tpu_custom_call" | custom-call | flops 8053063680 | bytes 14680064 | tf_op jit(solution)/shard_map/pallas_call | solution.py:520
  80.0 2.7 %shard_map.85 = (bf16[512,2048]{1,0:T(8,128)(2,1)}, bf16[512,2048]{1,0:T(8,128)(2,1)}, bf16[512,2048]{1,0:T(8,128)(2,1)}, f32[1,2048]{1,0:T(1,128)}) custom-call(bf16[512,2048]{1,0:T(8,128)(2,1)S(1)} %get-tuple-element.12.qg, bf16[512,2048]{1,0:T(8,128)(2,1)S(1)} %get-tuple-element.13.kg, bf16[512,2048]{1,0:T(8,128)(2,1)S(1)} %get-tuple-element.14.vg, ...), custom_call_target="tpu_custom_call" | custom-call | tf_op jit(solution)/shard_map/pallas_call | solution.py:563

commit v6 on v3

--- a/solution.py
+++ b/solution.py
@@ -62,7 +62,11 @@
         self.ch = self.piece // chunks
 
     def peer(self, d):
-        return lax.rem(self.i + d, self.g)
+        peer, bit = 0, 1
+        while bit < self.g:
+            peer = peer + lax.rem(self.i // bit + d // bit, 2) * bit
+            bit *= 2
+        return peer
 
     def rows(self, p, j):
         return pl.ds(pl.multiple_of(p * self.piece + j * self.ch, self.ch), self.ch)
@@ -154,7 +158,7 @@
         for p in reversed(order) if self.reverse else order:
             self.outs[p, part] = running
             running = running + self.slots[p, part]
-        for d in range(1, self.g):
+        for d in reversed(range(1, self.g)):
             self.hand(d, j).start()
         self.result[self.rows(self.i, j)] = self.outs[self.i, part]
 
@@ -182,7 +186,7 @@
     q, k, v, cot, do, att, kg_l, vg_l, w_top, w_low,
     own, slots, carry, fwd, before, outs, result,
     sq, cr, stats, gp, gz,
-    in_sem, a_send, a_recv, z_send, z_recv, b_send, b_recv,
+    in_sem, head_sem, a_send, a_recv, z_send, z_recv, b_send, b_recv,
     f_send, f_recv, g_send, g_recv, h_send, h_recv,
 ):
     rows, width = q.shape
@@ -193,12 +197,15 @@
     mine = lax.axis_index("fsdp")
     z, i = me // g, lax.rem(me, g)
 
+    def load_head(at, head):
+        src, dst = ((k_hbm, k), (v_hbm, v))[at]
+        cols = cols_of(head)
+        return pltpu.make_async_copy(src.at[:, cols], dst.at[:, cols], head_sem.at[at, head])
+
     loads = [
         pltpu.make_async_copy(src, dst, in_sem.at[at])
-        for at, (src, dst) in enumerate(((k_hbm, k), (v_hbm, v), (q_hbm, q), (c_hbm, cot)))
+        for at, (src, dst) in enumerate(((q_hbm, q), (c_hbm, cot)))
     ]
-    for load in loads:
-        load.start()
 
     barrier = pltpu.get_barrier_semaphore()
     for d in range(1, g):
@@ -223,7 +230,7 @@
 
     def make_states(scan, state_of):
         def turn(t, _):
-            j, d = t // g, lax.rem(t + 1, g)
+            j, d = t // g, g - 1 - lax.rem(t, g)
             p = scan.peer(d)
             state = state_of(p * per + j)
             scan.own[scan.rows(p, j)] = state
@@ -272,11 +279,24 @@
         at = pl.ds(pl.multiple_of(head * HEAD_DIM, HEAD_DIM), HEAD_DIM)
         return scan.result[at].astype(BF16)
 
+    def begin(t, _):
+        head = scans[0].peer(g - 1 - lax.rem(t, g)) * per + t // g if per else t
+        load_head(0, head).start()
+        load_head(1, head).start()
+        return 0
+
+    lax.fori_loop(0, heads, begin, 0)
+    for load in loads:
+        load.start()
+    pl.semaphore_wait(barrier, (g - 1) + (m - 1) + (fs - 1))
+
+    def state(head):
+        load_head(0, head).wait()
+        load_head(1, head).wait()
+        return dot_atb(k[:, cols_of(head)], v[:, cols_of(head)])
+
+    make_states(scans[0], state)
     loads[0].wait()
-    loads[1].wait()
-    pl.semaphore_wait(barrier, (g - 1) + (m - 1) + (fs - 1))
-    make_states(scans[0], lambda head: dot_atb(k[:, cols_of(head)], v[:, cols_of(head)]))
-    loads[2].wait()
 
     top, low = pl.ds(0, half), pl.ds(half, half)
 
@@ -317,7 +337,7 @@
                 scan.process(j)
 
     beside(scans[0], inside, 2, 1)
-    loads[3].wait()
+    loads[1].wait()
 
     sq[...] = jnp.zeros_like(sq)
     cr[...] = jnp.zeros_like(cr)
@@ -497,7 +517,8 @@
                 pltpu.VMEM((fs, rows, HEAD_DIM), F32),
                 pltpu.VMEM((g, 1, width), F32),
                 pltpu.VMEM((m, 1, width), F32),
-                dma((4,)),
+                dma((2,)),
+                dma((2, heads)),
                 dma((2, g, chunks)),
                 dma((2, g, chunks)),
                 dma((2, levels, max(m // 2, 1), chunks)),

time: 77 us -> 77.8 us (1.010)
  Pallas kernels: 76.1 us -> 76.9 us
    pallas_call x1, Pallas kernels: 73.4 us -> 74.2 us  [shards(): pl.pallas_call(functools.partial(kernel, n, g, fs, chunks), out_shape=(he...]
where the time goes in v6:
time: 77.8 us; the launch traced here: 77.6 us
  Pallas kernels  76.9 us (99%)
    pallas_call x1, Pallas kernels, shards(): pl.pallas_call(functools.partial(kernel, n, g, fs, chunks), out_shape=(he...  74.2 us
    pallas_call x1, Pallas kernels, shards(): pl.pallas_call(store, out_shape=(big, big, big, small), in_specs=[any_spa...  2.74 us

profile of v6, /device:TPU:0, one launch (start us, length us, event | category | flops | bytes accessed | tf_op | source)
XLA Modules:
  0.0 77.6 jit_solution(7293011598729044877)
XLA Ops:
  0.6 74.2 %shard_map.84 = (bf16[512,2048]{1,0:T(8,128)(2,1)S(1)}, bf16[512,2048]{1,0:T(8,128)(2,1)S(1)}, bf16[512,2048]{1,0:T(8,128)(2,1)S(1)}, f32[1,2048]{1,0:T(1,128)S(1)}) custom-call(bf16[512,2048]{1,0:T(8,128)(2,1)} %q_hbm.1, bf16[512,2048]{1,0:T(8,128)(2,1)} %k_hbm.1, bf16[512,2048]{1,0:T(8,128)(2,1)} %v_hbm.1, bf16[512,2048]{1,0:T(8,128)(2,1)} %c_hbm.1, ...), custom_call_target="tpu_custom_call" | custom-call | flops 8053063680 | bytes 14680064 | tf_op jit(solution)/shard_map/pallas_call | solution.py:498
  74.8 2.7 %shard_map.85 = (bf16[512,2048]{1,0:T(8,128)(2,1)}, bf16[512,2048]{1,0:T(8,128)(2,1)}, bf16[512,2048]{1,0:T(8,128)(2,1)}, f32[1,2048]{1,0:T(1,128)}) custom-call(bf16[512,2048]{1,0:T(8,128)(2,1)S(1)} %get-tuple-element.12.qg, bf16[512,2048]{1,0:T(8,128)(2,1)S(1)} %get-tuple-element.13.kg, bf16[512,2048]{1,0:T(8,128)(2,1)S(1)} %get-tuple-element.14.vg, ...), custom_call_target="tpu_custom_call" | custom-call | tf_op jit(solution)/shard_map/pallas_call | solution.py:542

commit v7 on v3

--- a/solution.py
+++ b/solution.py
@@ -316,7 +316,7 @@
                 scan.gather(j)
                 scan.process(j)
 
-    beside(scans[0], inside, 2, 1)
+    beside(scans[0], inside, 2, 2)
     loads[3].wait()
 
     sq[...] = jnp.zeros_like(sq)
@@ -410,7 +410,7 @@
         vg_l[top, cols] = dot_ab(w_top[head], dh)
         vg_l[low, cols] = dot_ab(w_low[head], d1)
 
-    beside(scans[1], backward, 1, 1)
+    beside(scans[1], backward, 1, 2)
 
     for d in range(1, g):
         gain_near(d, lax.rem(i + d, g)).wait_recv()

time: 77 us -> 74.9 us (0.973)
  Pallas kernels: 76.1 us -> 74.1 us
    pallas_call x1, Pallas kernels: 73.4 us -> 71.3 us  [shards(): pl.pallas_call(functools.partial(kernel, n, g, fs, chunks), out_shape=(he...]
where the time goes in v7:
time: 74.9 us; the launch traced here: 74.7 us
  Pallas kernels  74.1 us (99%)
    pallas_call x1, Pallas kernels, shards(): pl.pallas_call(functools.partial(kernel, n, g, fs, chunks), out_shape=(he...  71.3 us
    pallas_call x1, Pallas kernels, shards(): pl.pallas_call(store, out_shape=(big, big, big, small), in_specs=[any_spa...  2.74 us

profile of v7, /device:TPU:0, one launch (start us, length us, event | category | flops | bytes accessed | tf_op | source)
XLA Modules:
  0.0 74.7 jit_solution(6265077638825287151)
XLA Ops:
  0.6 71.3 %shard_map.84 = (bf16[512,2048]{1,0:T(8,128)(2,1)S(1)}, bf16[512,2048]{1,0:T(8,128)(2,1)S(1)}, bf16[512,2048]{1,0:T(8,128)(2,1)S(1)}, f32[1,2048]{1,0:T(1,128)S(1)}) custom-call(bf16[512,2048]{1,0:T(8,128)(2,1)} %q_hbm.1, bf16[512,2048]{1,0:T(8,128)(2,1)} %k_hbm.1, bf16[512,2048]{1,0:T(8,128)(2,1)} %v_hbm.1, bf16[512,2048]{1,0:T(8,128)(2,1)} %c_hbm.1, ...), custom_call_target="tpu_custom_call" | custom-call | flops 8053063680 | bytes 14680064 | tf_op jit(solution)/shard_map/pallas_call | solution.py:478
  72.0 2.7 %shard_map.85 = (bf16[512,2048]{1,0:T(8,128)(2,1)}, bf16[512,2048]{1,0:T(8,128)(2,1)}, bf16[512,2048]{1,0:T(8,128)(2,1)}, f32[1,2048]{1,0:T(1,128)}) custom-call(bf16[512,2048]{1,0:T(8,128)(2,1)S(1)} %get-tuple-element.12.qg, bf16[512,2048]{1,0:T(8,128)(2,1)S(1)} %get-tuple-element.13.kg, bf16[512,2048]{1,0:T(8,128)(2,1)S(1)} %get-tuple-element.14.vg, ...), custom_call_target="tpu_custom_call" | custom-call | tf_op jit(solution)/shard_map/pallas_call | solution.py:521
